TPU v7x, 32 devices: a whole 2x2x4 slice. The times are simulated.
32 devices in a mesh: pool: 8 (over z, y), head: 4 (over x, core).
Axes of the slice: x: 2, y: 2, z: 4, core: 2. Of those that a mesh axis runs over, the one named last changes fastest.
Arguments:
- queries: bfloat16 [8, 256, 8192], P('pool', None, 'head'), may hold values from -6 to 6
- new_kv: bfloat16 [8, 256, 2048], P('pool', None, 'head'), may hold values from -6 to 6
- pool: bfloat16 [256, 256, 2048], P('pool', None, 'head'), may hold values from -6 to 6
- page_owner: int32 [8, 32], replicated, may hold values from 0 to 7, as said below
- page_slot: int32 [8, 32], replicated, may hold values from 0 to 31, as said below
- cached_len: int32 [8], replicated, may hold values from 1 to 8192, as said below
Outputs:
- attended: bfloat16 [8, 256, 8192], P('pool', None, 'head')
Inputs may be any that keep to these rules, and one draw needn't show every extreme that they name: `page_owner`: each of the 32 entries of a row is the owner of that page of the request; every owner holds exactly 4 entries of each row. Pairs (page_owner, page_slot) are distinct over all requests and pages. Request r uses its first ceil(cached_len[r] / 256) pages; some request has exactly 8192 cached tokens.
All inputs are finite; a program needn't handle non-finite values.
Results may differ from a plain program's by a relative error of at most 0.0075.
Values may be sent and summed in bfloat16 or wider, within the bound.
A program may use at most 64 MiB of HBM per device.

v0:
```python
import functools
import math

import jax
import jax.numpy as jnp
from jax import lax
from jax.experimental import pallas as pl
from jax.experimental.pallas import tpu as pltpu
from jax.sharding import PartitionSpec as P

HD = 128
MESH = pl.DeviceIdType.MESH


def partner_of(me, k):
    out = me
    bit = 1
    while bit <= k:
        if k & bit:
            out = out + bit * (1 - 2 * ((me // bit) % 2))
        bit *= 2
    return out


def collect_kernel(count, slot_ref, pool_ref, out_ref, sems):
    def start(i, carry):
        pltpu.make_async_copy(pool_ref.at[slot_ref[i]], out_ref.at[i], sems.at[i]).start()
        return carry

    def finish(i, carry):
        pltpu.make_async_copy(pool_ref.at[0], out_ref.at[i], sems.at[i]).wait()
        return carry

    lax.fori_loop(0, count, start, 0)
    lax.fori_loop(0, count, finish, 0)


def attend_kernel(
    n, cap, valid_ref, q_ref, fresh_ref, outgoing_ref, out_ref,
    recv, peak, total, acc, send_sems, recv_sems,
):
    me = lax.axis_index("pool")
    heads, new_tok, _ = q_ref.shape
    page_len = recv.shape[1] // cap
    kv_dev = fresh_ref.shape[1] // (2 * HD)
    group = heads // kv_dev
    scale2 = math.log2(math.e) / math.sqrt(HD)

    barrier = pltpu.get_barrier_semaphore()
    for k in range(1, n):
        pl.semaphore_signal(
            barrier, inc=1, device_id={"pool": partner_of(me, k)}, device_id_type=MESH
        )
    own_copy = pltpu.make_async_copy(outgoing_ref.at[0], recv.at[0], recv_sems.at[0])
    own_copy.start()
    pl.semaphore_wait(barrier, n - 1)
    sends = []
    for k in range(n - 1, 0, -1):
        send = pltpu.make_async_remote_copy(
            src_ref=outgoing_ref.at[k],
            dst_ref=recv.at[k],
            send_sem=send_sems.at[k],
            recv_sem=recv_sems.at[k],
            device_id={"pool": partner_of(me, k)},
            device_id_type=MESH,
        )
        send.start()
        sends.append(send)

    def scores_of(keys, h):
        return lax.dot_general(
            keys, q_ref[h], (((1,), (1,)), ((), ())), preferred_element_type=jnp.float32
        )

    def weigh(values, weights):
        return lax.dot_general(
            values, weights, (((0,), (0,)), ((), ())), preferred_element_type=jnp.float32
        )

    key_no = lax.broadcasted_iota(jnp.int32, (new_tok, new_tok), 0)
    tok_no = lax.broadcasted_iota(jnp.int32, (new_tok, new_tok), 1)
    for g in range(kv_dev):
        keys = fresh_ref[:, 2 * g * HD : (2 * g + 1) * HD]
        values = fresh_ref[:, (2 * g + 1) * HD : (2 * g + 2) * HD]

        def first(i, carry):
            h = g * group + i
            s = jnp.where(key_no <= tok_no, scores_of(keys, h), -jnp.inf)
            top = jnp.max(s, axis=0, keepdims=True)
            w = jnp.exp2((s - top) * scale2)
            peak[h] = top
            total[h] = jnp.sum(w, axis=0, keepdims=True)
            acc[h] = weigh(values, w.astype(jnp.bfloat16))
            return carry

        lax.fori_loop(0, group, first, 0)

    rows = lax.broadcasted_iota(jnp.int32, (page_len, new_tok), 0)

    def attend(k):
        limits = [valid_ref[k * cap + j] for j in range(cap)]
        for g in range(kv_dev):

            def one_head(h):
                keys = recv[k, :, 2 * g * HD : (2 * g + 1) * HD]
                values = recv[k, :, (2 * g + 1) * HD : (2 * g + 2) * HD]
                s = scores_of(keys, h)
                s = jnp.concatenate(
                    [
                        jnp.where(
                            rows < limits[j], s[j * page_len : (j + 1) * page_len], -jnp.inf
                        )
                        for j in range(cap)
                    ],
                    axis=0,
                )
                before = peak[h]
                top = jnp.maximum(before, jnp.max(s, axis=0, keepdims=True))
                w = jnp.exp2((s - top) * scale2)
                factor = jnp.exp2((before - top) * scale2)
                peak[h] = top
                total[h] = total[h] * factor + jnp.sum(w, axis=0, keepdims=True)
                acc[h] = acc[h] * factor + weigh(values, w.astype(jnp.bfloat16))

            def two_heads(i, carry):
                one_head(g * group + 2 * i)
                one_head(g * group + 2 * i + 1)
                return carry

            lax.fori_loop(0, group // 2, two_heads, 0)

    own_copy.wait()
    attend(0)

    def one_block(k, carry):
        pltpu.make_async_copy(recv.at[k], recv.at[k], recv_sems.at[k]).wait()
        attend(k)
        return carry

    lax.fori_loop(1, n, one_block, 0)
    for h in range(heads):
        out_ref[:, h * HD : (h + 1) * HD] = (acc[h] / total[h]).T.astype(out_ref.dtype)
    for send in sends:
        send.wait_send()


def on_device(queries, new_kv, pool, page_owner, page_slot, cached_len):
    n = lax.axis_size("pool")
    me = lax.axis_index("pool")
    page_len, width = pool.shape[1], pool.shape[2]
    max_pages = page_owner.shape[1]
    cap = max_pages // n
    new_tok = queries.shape[1]
    heads = queries.shape[2] // HD
    page_no = jnp.arange(max_pages, dtype=jnp.int32)
    places = jnp.arange(cap, dtype=jnp.int32)
    partners = jnp.bitwise_xor(me, jnp.arange(n, dtype=jnp.int32))

    same = (page_owner[:, :, None] == page_owner[:, None, :]) & (
        page_no[None, None, :] < page_no[None, :, None]
    )
    rank = jnp.sum(same.astype(jnp.int32), axis=2)
    mine = (page_owner == me)[:, None, :] & (rank[:, None, :] == places[None, :, None])
    slots = jnp.sum(jnp.where(mine, page_slot[:, None, :], 0), axis=2)
    pick = (partners[:, None] == jnp.arange(n, dtype=jnp.int32)[None, :]).astype(jnp.int32)
    slots = jnp.sum(pick[:, :, None] * slots[None, :, :], axis=1).reshape(-1)

    is_me = jnp.arange(n, dtype=jnp.int32) == me
    my_owner = jnp.sum(jnp.where(is_me[:, None], page_owner, 0), axis=0)
    my_rank = jnp.sum(jnp.where(is_me[:, None], rank, 0), axis=0)
    my_len = jnp.sum(jnp.where(is_me, cached_len, 0))
    seen = jnp.clip(my_len - page_no * page_len, 0, page_len)
    hit = (my_owner[None, None, :] == partners[:, None, None]) & (
        my_rank[None, None, :] == places[None, :, None]
    )
    valid = jnp.sum(jnp.where(hit, seen[None, None, :], 0), axis=2).reshape(-1)

    outgoing = pl.pallas_call(
        functools.partial(collect_kernel, n * cap),
        out_shape=jax.ShapeDtypeStruct((n * cap, page_len, width), pool.dtype),
        in_specs=[pl.BlockSpec(memory_space=pltpu.SMEM), pl.BlockSpec(memory_space=pl.ANY)],
        out_specs=pl.BlockSpec(memory_space=pl.ANY),
        scratch_shapes=[pltpu.SemaphoreType.DMA((n * cap,))],
        name="collect",
    )(slots, pool)
    outgoing = outgoing.reshape(n, cap * page_len, width)

    q_heads = queries[0].reshape(new_tok, heads, HD).transpose(1, 0, 2)
    vmem = pl.BlockSpec(memory_space=pltpu.VMEM)
    out = pl.pallas_call(
        functools.partial(attend_kernel, n, cap),
        out_shape=jax.ShapeDtypeStruct((new_tok, heads * HD), jnp.bfloat16),
        in_specs=[
            pl.BlockSpec(memory_space=pltpu.SMEM), vmem, vmem, pl.BlockSpec(memory_space=pl.ANY)
        ],
        out_specs=vmem,
        scratch_shapes=[
            pltpu.VMEM((n, cap * page_len, width), jnp.bfloat16),
            pltpu.VMEM((heads, 1, new_tok), jnp.float32),
            pltpu.VMEM((heads, 1, new_tok), jnp.float32),
            pltpu.VMEM((heads, HD, new_tok), jnp.float32),
            pltpu.SemaphoreType.DMA((n,)),
            pltpu.SemaphoreType.DMA((n,)),
        ],
        compiler_params=pltpu.CompilerParams(
            collective_id=0, has_side_effects=True, vmem_limit_bytes=48 * 1024 * 1024
        ),
        name="attend",
    )(valid, q_heads, new_kv[0], outgoing)
    return out[None]


def solution(mesh):
    split = P("pool", None, "head")
    return jax.shard_map(
        on_device,
        mesh=mesh,
        in_specs=(split, split, split, P(), P(), P()),
        out_specs=split,
        check_vma=False,
    )
```

profile of v0, /device:TPU:0, one launch (start us, length us, event | category | flops | bytes accessed | tf_op | source)
XLA Modules:
  0.0 519.8 jit_solution(16379461961007022876)
XLA Ops:
  0.0 0.7 broadcast_compare_fusion
  0.7 1.3 select_reduce_fusion.4
  2.0 0.7 subtract_clamp_fusion
  2.6 0.1 fusion.1
  2.7 1.1 convert_reduce_fusion
  3.8 0.8 select_reduce_fusion.3
  4.6 0.8 select_reduce_fusion
  5.4 0.2 multiply_reduce_fusion
  5.5 0.1 broadcast_compare_fusion.1
  5.6 0.2 select_reduce_fusion.1
  5.8 0.1 copy.9
  5.9 0.1 reshape.123.valid_ref
  6.0 0.1 copy.12
  6.0 0.6 reshape.124.slot_ref
  6.6 1.5 copy.10
  8.1 0.7 copy.11
  8.8 0.0 copy-start
  8.8 256.3 %collect.1 = bf16[32,256,512]{2,1,0:T(8,128)(2,1)} custom-call(s32[32]{0:T(128)} %reshape.124.slot_ref, bf16[32,256,512]{2,1,0:T(8,128)(2,1)} %pool_ref.1), custom_call_target="tpu_custom_call" | custom-call | tf_op jit(solution)/shard_map/collect/pallas_call | solution.py:178
  265.1 0.0 copy-done
  265.1 253.7 %attend.1 = bf16[256,2048]{1,0:T(8,128)(2,1)S(1)} custom-call(s32[32]{0:T(128)S(1)} %reshape.123.valid_ref, bf16[16,256,128]{2,1,0:T(8,128)(2,1)S(1)} %bitcast.5, bf16[256,512]{1,0:T(8,128)(2,1)S(1)} %bitcast.7, bf16[8,1024,512]{2,1,0:T(8,128)(2,1)} %bitcast.8), custom_call_target="tpu_custom_call" | custom-call | tf_op jit(solution)/shard_map/attend/pallas_call | solution.py:190
  518.9 1.0 copy.14
  (3 shorter events, 0.0 us)
Async XLA Ops:
  8.8 256.3 %copy-start = (bf16[1,256,512]{2,1,0:T(8,128)(2,1)S(1)}, bf16[1,256,512]{2,1,0:T(8,128)(2,1)}, u32[]{:S(2)}) copy-start(bf16[1,256,512]{2,1,0:T(8,128)(2,1)} %param.7) | copy-start | bytes 786436
where the time goes:
time: 520 us
  Pallas kernels  510 us (98%)
  other arithmetic  5.77 us (1%)
    pallas_call x1, Pallas kernels, on_device(): pl.pallas_call(functools.partial(collect_kernel, n * cap), out_shape=jax....  256 us
    pallas_call x1, Pallas kernels, on_device(): pl.pallas_call(functools.partial(attend_kernel, n, cap), out_shape=jax.Sh...  254 us

commit v1 on v0

--- a/solution.py
+++ b/solution.py
@@ -12,35 +12,31 @@
 MESH = pl.DeviceIdType.MESH
 
 
-def partner_of(me, k):
+def partner_of(me, k, n):
     out = me
     bit = 1
-    while bit <= k:
-        if k & bit:
-            out = out + bit * (1 - 2 * ((me // bit) % 2))
+    while bit < n:
+        out = out + bit * ((k // bit) % 2) * (1 - 2 * ((me // bit) % 2))
         bit *= 2
     return out
 
 
-def collect_kernel(count, slot_ref, pool_ref, out_ref, sems):
-    def start(i, carry):
-        pltpu.make_async_copy(pool_ref.at[slot_ref[i]], out_ref.at[i], sems.at[i]).start()
-        return carry
-
-    def finish(i, carry):
-        pltpu.make_async_copy(pool_ref.at[0], out_ref.at[i], sems.at[i]).wait()
-        return carry
-
-    lax.fori_loop(0, count, start, 0)
-    lax.fori_loop(0, count, finish, 0)
+def collect_kernel(slot_ref, *refs):
+    out_ref = refs[-1]
+    for j, page_ref in enumerate(refs[:-1]):
+        out_ref[j] = page_ref[0]
+
+
+def page_spec(step, j, page_len, width):
+    return pl.BlockSpec((1, page_len, width), lambda i, slot_ref: (slot_ref[i * step + j], 0, 0))
 
 
 def attend_kernel(
     n, cap, valid_ref, q_ref, fresh_ref, outgoing_ref, out_ref,
-    recv, peak, total, acc, send_sems, recv_sems,
+    recv, turned, peak, total, acc, send_sems, recv_sems,
 ):
     me = lax.axis_index("pool")
-    heads, new_tok, _ = q_ref.shape
+    heads, _, new_tok = q_ref.shape
     page_len = recv.shape[1] // cap
     kv_dev = fresh_ref.shape[1] // (2 * HD)
     group = heads // kv_dev
@@ -49,39 +45,41 @@
     barrier = pltpu.get_barrier_semaphore()
     for k in range(1, n):
         pl.semaphore_signal(
-            barrier, inc=1, device_id={"pool": partner_of(me, k)}, device_id_type=MESH
+            barrier, inc=1, device_id={"pool": partner_of(me, k, n)}, device_id_type=MESH
         )
     own_copy = pltpu.make_async_copy(outgoing_ref.at[0], recv.at[0], recv_sems.at[0])
     own_copy.start()
     pl.semaphore_wait(barrier, n - 1)
-    sends = []
-    for k in range(n - 1, 0, -1):
-        send = pltpu.make_async_remote_copy(
+
+    def send_of(k):
+        return pltpu.make_async_remote_copy(
             src_ref=outgoing_ref.at[k],
             dst_ref=recv.at[k],
             send_sem=send_sems.at[k],
             recv_sem=recv_sems.at[k],
-            device_id={"pool": partner_of(me, k)},
+            device_id={"pool": partner_of(me, k, n)},
             device_id_type=MESH,
         )
-        send.start()
-        sends.append(send)
+
+    half, late = n // 2, n // 4
+    for k in [*range(half, n - late), *range(half - 1, 0, -1)]:
+        send_of(k).start()
 
     def scores_of(keys, h):
         return lax.dot_general(
-            keys, q_ref[h], (((1,), (1,)), ((), ())), preferred_element_type=jnp.float32
+            keys, q_ref[h], (((1,), (0,)), ((), ())), preferred_element_type=jnp.float32
         )
 
     def weigh(values, weights):
         return lax.dot_general(
-            values, weights, (((0,), (0,)), ((), ())), preferred_element_type=jnp.float32
+            values, weights, (((1,), (0,)), ((), ())), preferred_element_type=jnp.float32
         )
 
     key_no = lax.broadcasted_iota(jnp.int32, (new_tok, new_tok), 0)
     tok_no = lax.broadcasted_iota(jnp.int32, (new_tok, new_tok), 1)
     for g in range(kv_dev):
         keys = fresh_ref[:, 2 * g * HD : (2 * g + 1) * HD]
-        values = fresh_ref[:, (2 * g + 1) * HD : (2 * g + 2) * HD]
+        values = fresh_ref[:, (2 * g + 1) * HD : (2 * g + 2) * HD].T
 
         def first(i, carry):
             h = g * group + i
@@ -100,10 +98,11 @@
     def attend(k):
         limits = [valid_ref[k * cap + j] for j in range(cap)]
         for g in range(kv_dev):
+            turned[...] = recv[k, :, (2 * g + 1) * HD : (2 * g + 2) * HD].T
 
             def one_head(h):
                 keys = recv[k, :, 2 * g * HD : (2 * g + 1) * HD]
-                values = recv[k, :, (2 * g + 1) * HD : (2 * g + 2) * HD]
+                values = turned[...]
                 s = scores_of(keys, h)
                 s = jnp.concatenate(
                     [
@@ -134,14 +133,19 @@
 
     def one_block(k, carry):
         pltpu.make_async_copy(recv.at[k], recv.at[k], recv_sems.at[k]).wait()
+
+        @pl.when((k >= half) & (k < half + late))
+        def _():
+            send_of(k + late).start()
+
         attend(k)
         return carry
 
     lax.fori_loop(1, n, one_block, 0)
     for h in range(heads):
         out_ref[:, h * HD : (h + 1) * HD] = (acc[h] / total[h]).T.astype(out_ref.dtype)
-    for send in sends:
-        send.wait_send()
+    for k in range(1, n):
+        send_of(k).wait_send()
 
 
 def on_device(queries, new_kv, pool, page_owner, page_slot, cached_len):
@@ -175,17 +179,22 @@
     )
     valid = jnp.sum(jnp.where(hit, seen[None, None, :], 0), axis=2).reshape(-1)
 
+    step = math.gcd(n * cap, 4)
     outgoing = pl.pallas_call(
-        functools.partial(collect_kernel, n * cap),
+        collect_kernel,
         out_shape=jax.ShapeDtypeStruct((n * cap, page_len, width), pool.dtype),
-        in_specs=[pl.BlockSpec(memory_space=pltpu.SMEM), pl.BlockSpec(memory_space=pl.ANY)],
-        out_specs=pl.BlockSpec(memory_space=pl.ANY),
-        scratch_shapes=[pltpu.SemaphoreType.DMA((n * cap,))],
+        grid_spec=pltpu.PrefetchScalarGridSpec(
+            num_scalar_prefetch=1,
+            grid=(n * cap // step,),
+            in_specs=[page_spec(step, j, page_len, width) for j in range(step)],
+            out_specs=pl.BlockSpec((step, page_len, width), lambda i, slot_ref: (i, 0, 0)),
+        ),
+        compiler_params=pltpu.CompilerParams(vmem_limit_bytes=16 * 1024 * 1024),
         name="collect",
-    )(slots, pool)
+    )(slots, *([pool] * step))
     outgoing = outgoing.reshape(n, cap * page_len, width)
 
-    q_heads = queries[0].reshape(new_tok, heads, HD).transpose(1, 0, 2)
+    q_heads = queries[0].reshape(new_tok, heads, HD).transpose(1, 2, 0)
     vmem = pl.BlockSpec(memory_space=pltpu.VMEM)
     out = pl.pallas_call(
         functools.partial(attend_kernel, n, cap),
@@ -196,6 +205,7 @@
         out_specs=vmem,
         scratch_shapes=[
             pltpu.VMEM((n, cap * page_len, width), jnp.bfloat16),
+            pltpu.VMEM((HD, cap * page_len), jnp.bfloat16),
             pltpu.VMEM((heads, 1, new_tok), jnp.float32),
             pltpu.VMEM((heads, 1, new_tok), jnp.float32),
             pltpu.VMEM((heads, HD, new_tok), jnp.float32),

time: 520 us -> 216 us (0.42)
  the two profiles are of different devices: /device:TPU:0 before, /device:TPU:11 now
where the time goes in v1:
time: 216 us
  Pallas kernels  201 us (93%)
  local copies, waits for them, and re-layouts  9.38 us (4%)
  other arithmetic  5.77 us (3%)
    pallas_call x1, Pallas kernels, on_device(): pl.pallas_call(functools.partial(attend_kernel, n, cap), out_shape=jax.Sh...  199 us
    unnamed x8, local copies, waits for them, and re-layouts  9.05 us

profile of v1, /device:TPU:11, one launch (start us, length us, event | category | flops | bytes accessed | tf_op | source)
XLA Modules:
  0.0 215.9 jit_solution(14020975269846920719)
XLA Ops:
  0.0 0.7 broadcast_compare_fusion
  0.7 1.3 select_reduce_fusion.4
  2.0 0.7 subtract_clamp_fusion
  2.6 0.1 fusion.1
  2.7 1.1 convert_reduce_fusion
  3.8 0.8 select_reduce_fusion.3
  4.6 0.8 select_reduce_fusion
  5.4 0.2 multiply_reduce_fusion
  5.5 0.1 broadcast_compare_fusion.1
  5.6 0.2 select_reduce_fusion.1
  5.8 0.1 copy.9
  5.9 0.1 reshape.123.valid_ref
  6.0 0.1 copy.11
  6.0 0.1 reshape.124.slot_ref
  6.1 1.5 copy.10
  7.6 0.0 copy-start
  7.6 3.4 %copy-done = bf16[32,256,512]{2,1,0:T(8,128)(2,1)S(1)} copy-done((bf16[32,256,512]{2,1,0:T(8,128)(2,1)S(1)}, bf16[32,256,512]{2,1,0:T(8,128)(2,1)}, u32[]{:S(2)}) %copy-start) | copy-done | bytes 8388632
  11.0 0.0 copy-start.2
  11.0 1.2 collect.1
  12.2 0.0 copy-start.1
  12.2 3.2 %copy-done.1 = bf16[32,256,512]{2,1,0:T(8,128)(2,1)} copy-done((bf16[32,256,512]{2,1,0:T(8,128)(2,1)}, bf16[32,256,512]{2,1,0:T(8,128)(2,1)S(1)}, u32[]{:S(2)}) %copy-start.1) | copy-done | bytes 8388632
  15.4 0.0 copy-done.2
  15.4 199.4 %attend.1 = bf16[256,2048]{1,0:T(8,128)(2,1)S(1)} custom-call(s32[32]{0:T(128)S(1)} %reshape.123.valid_ref, bf16[16,128,256]{2,1,0:T(8,128)(2,1)S(1)} %bitcast.7, bf16[256,512]{1,0:T(8,128)(2,1)S(1)} %bitcast.9, bf16[8,1024,512]{2,1,0:T(8,128)(2,1)} %bitcast.6), custom_call_target="tpu_custom_call" | custom-call | tf_op jit(solution)/shard_map/attend/pallas_call | solution.py:199
  214.9 1.0 copy.13
  (3 shorter events, 0.0 us)
Async XLA Ops:
  7.6 3.4 %copy-start = (bf16[32,256,512]{2,1,0:T(8,128)(2,1)S(1)}, bf16[32,256,512]{2,1,0:T(8,128)(2,1)}, u32[]{:S(2)}) copy-start(bf16[32,256,512]{2,1,0:T(8,128)(2,1)} %refs_3_.1) | copy-start | bytes 25165828
  11.0 4.5 %copy-start.2 = (bf16[1,256,512]{2,1,0:T(8,128)(2,1)S(1)}, bf16[1,256,512]{2,1,0:T(8,128)(2,1)}, u32[]{:S(2)}) copy-start(bf16[1,256,512]{2,1,0:T(8,128)(2,1)} %param.7) | copy-start | bytes 786436
  12.2 3.2 %copy-start.1 = (bf16[32,256,512]{2,1,0:T(8,128)(2,1)}, bf16[32,256,512]{2,1,0:T(8,128)(2,1)S(1)}, u32[]{:S(2)}) copy-start(bf16[32,256,512]{2,1,0:T(8,128)(2,1)S(1)} %collect.1) | copy-start | bytes 25165828
